TPU v7x, 512 devices: a whole 4x4x16 slice. The times are simulated.
512 devices in a mesh: tm: 32 (over z_lo, y, core), rows: 16 (over z_hi, x).
Axes of the slice: x: 4, y: 4, z: 16 (z_hi: 4, z_lo: 4; z = z_hi * 4 + z_lo), core: 2. Of those that a mesh axis runs over, the one named last changes fastest.
Arguments:
- video: bfloat16 [64, 64, 120, 128], P('tm', 'rows'), may hold values from -6 to 6
- norm_gain: bfloat16 [128], replicated, may hold values from 0.099609375 to 1.8984375
- conv_first: bfloat16 [3, 3, 3, 128, 128], replicated, may hold values from -0.109375 to 0.109375
- conv_second: bfloat16 [3, 3, 3, 128, 128], replicated, may hold values from -0.109375 to 0.109375
- attn_gain: bfloat16 [128], replicated, may hold values from 0.099609375 to 1.8984375
- query_weight: bfloat16 [128, 128], replicated, may hold values from -2 to 2
- key_weight: bfloat16 [128, 128], replicated, may hold values from -2 to 2
- value_weight: bfloat16 [128, 128], replicated, may hold values from -0.5 to 0.5
- out_weight: bfloat16 [128, 128], replicated, may hold values from -0.5 to 0.5
Outputs:
- result: bfloat16 [64, 64, 120, 128], P('tm', 'rows')
All inputs are finite; a program needn't handle non-finite values.
Results may differ from a plain program's by a relative error of at most 0.013.
Values may be sent and summed in bfloat16 or wider, within the bound.
A program may use at most 64 MiB of HBM per device.

v0:
```python
import jax
import jax.numpy as jnp
from jax import lax
from jax.sharding import PartitionSpec as P


def shifted(value, axis, steps):
    count = lax.axis_size(axis)
    leading, last = (max(0, -steps), min(count, count - steps))
    return lax.ppermute(value, axis, [(source, source + steps) for source in range(leading, last)])


def with_halo(x, sides, width):
    for axis, dim in sides:
        size, length = (lax.axis_size(axis), x.shape[dim])
        up = [(i, (i + 1) % size) for i in range(size - 1)]
        down = [(j, i) for i, j in up]
        last = lax.slice_in_dim(x, length - width, length, axis=dim)
        leading = lax.slice_in_dim(x, 0, width, axis=dim)
        before = lax.ppermute(last, axis, up)
        after = lax.ppermute(leading, axis, down)
        x = jnp.concatenate([before, x, after], axis=dim)
    return x


def rms_norm(values, gain):
    wide = values.astype(jnp.float32)
    scale = lax.rsqrt(jnp.mean(wide * wide, axis=-1, keepdims=True) + 1e-06)
    return wide * scale * gain.astype(jnp.float32)


def convolve(field, kernel):
    frames, height, width, chans = field.shape
    earlier = shifted(field, "tm", 1)
    extended = jnp.concatenate([earlier, field], axis=0)
    padded = with_halo(extended, (("rows", 1),), 1)
    padded = jnp.pad(padded, ((0, 0), (0, 0), (1, 1), (0, 0)))
    total = jnp.zeros((frames * height * width, chans), jnp.float32)
    for shift_t in range(3):
        for shift_h in range(3):
            slab = padded[shift_t : shift_t + frames, shift_h : shift_h + height]
            joined = jnp.concatenate([slab[:, :, e : e + width] for e in range(3)], axis=-1)
            taps = kernel[shift_t, shift_h].reshape(3 * chans, chans)
            total = total + jnp.dot(
                joined.reshape(-1, 3 * chans), taps, preferred_element_type=jnp.float32
            )
    return total.reshape(frames, height, width, chans)


def block_scores(query, keys, query_first):
    chans = query.shape[-1]
    scores = jnp.einsum("fpc,gpc->fgp", query, keys, preferred_element_type=jnp.float32) / jnp.sqrt(
        jnp.float32(chans)
    )
    query_pos = query_first + jnp.arange(query.shape[0], dtype=jnp.int32)
    key_pos = jnp.arange(keys.shape[0], dtype=jnp.int32)
    allowed = (key_pos[None, :] <= query_pos[:, None])[:, :, None]
    tile_top = jnp.max(jnp.where(allowed, scores, jnp.float32(-1e30)), axis=1)
    return (scores, allowed, tile_top)


def absorb_block(carry, query, keys, values, query_first):
    top, total, acc = carry
    scores, allowed, tile_top = block_scores(query, keys, query_first)
    new_top = jnp.maximum(top, tile_top)
    weights = jnp.where(allowed, jnp.exp(scores - new_top[:, None, :]), jnp.float32(0.0))
    total = jnp.sum(weights, axis=1)
    update = jnp.einsum(
        "fgp,gpc->fpc", weights.astype(jnp.bfloat16), values, preferred_element_type=jnp.float32
    )
    acc = update
    return (new_top, total, acc)


def start_carry(frames, cells, chans):
    return (
        jnp.full((frames, cells), -1e30, jnp.float32),
        jnp.zeros((frames, cells), jnp.float32),
        jnp.zeros((frames, cells, chans), jnp.float32),
    )


def local(
    video,
    norm_gain,
    conv_first,
    conv_second,
    attn_gain,
    query_weight,
    key_weight,
    value_weight,
    out_weight,
):
    frames, height, width, chans = video.shape
    act = jax.nn.silu(rms_norm(video, norm_gain)).astype(jnp.bfloat16)
    mid = jax.nn.silu(convolve(act, conv_first)).astype(jnp.bfloat16)
    hidden = (video.astype(jnp.float32) + convolve(mid, conv_second)).astype(jnp.bfloat16)
    normed = rms_norm(hidden, attn_gain).astype(jnp.bfloat16)
    flat = normed.reshape(-1, chans)
    joined_weight = jnp.concatenate([query_weight, key_weight, value_weight], axis=1)
    projected = jnp.dot(flat, joined_weight, preferred_element_type=jnp.float32).astype(
        jnp.bfloat16
    )
    cells = height * width
    query = projected[:, :chans].reshape(frames, cells, chans)
    keys = projected[:, chans : 2 * chans].reshape(frames, cells, chans)
    values = projected[:, 2 * chans :].reshape(frames, cells, chans)
    query_first = lax.axis_index("tm") * frames
    top, total, acc = absorb_block(
        start_carry(frames, cells, chans),
        query,
        lax.all_gather(keys, "tm", axis=0, tiled=True),
        lax.all_gather(values, "tm", axis=0, tiled=True),
        query_first,
    )
    mixed = (acc / total[:, :, None]).astype(jnp.bfloat16)
    output = jnp.dot(mixed.reshape(-1, chans), out_weight, preferred_element_type=jnp.float32)
    result = hidden.reshape(-1, chans).astype(jnp.float32) + output
    return result.astype(jnp.bfloat16).reshape(frames, height, width, chans)


def solution(mesh):
    return jax.shard_map(
        local,
        mesh=mesh,
        in_specs=(P("tm", "rows", None, None), P(), P(), P(), P(), P(), P(), P(), P()),
        out_specs=P("tm", "rows", None, None),
        check_vma=False,
    )
```

profile of v0, /device:TPU:1, one launch (start us, length us, event | category | flops | bytes accessed | tf_op | source)
XLA Modules:
  0.0 247.9 jit_solution(13265334246154741844)
XLA Ops:
  6.5 1.2 fusion.26
  7.8 0.7 convert_element_type.47
  8.5 1.2 fusion.33
  9.6 4.6 %collective-permute-start = (bf16[2,4,120,128]{3,2,1,0:T(8,128)(2,1)S(1)}, bf16[2,4,120,128]{3,2,1,0:T(8,128)(2,1)S(1)}, u32[]{:S(2)}, u32[]{:S(2)}) collective-permute-start(bf16[2,4,120,128]{3,2,1,0:T(8,128)(2,1)S(1)} %fusion.33), channel_id=1, source_target_pairs={{0,16},{16,32},{32,48},{48,64},{64,80},{80,96},{96,112},{112,128},... | collective-permute-start | bytes 737288 | tf_op jit(solution)/shard_map/ppermute | solution.py:10
  14.2 4.6 %collective-permute-done = bf16[2,4,120,128]{3,2,1,0:T(8,128)(2,1)S(1)} collective-permute-done((bf16[2,4,120,128]{3,2,1,0:T(8,128)(2,1)S(1)}, bf16[2,4,120,128]{3,2,1,0:T(8,128)(2,1)S(1)}, u32[]{:S(2)}, u32[]{:S(2)}) %collective-permute-start) | collective-permute-done | bytes 245792 | tf_op jit(solution)/shard_map/ppermute | solution.py:10
  18.8 1.7 collective-permute-start.1
  20.5 1.3 collective-permute-start.2
  21.9 1.7 collective-permute-done.1
  23.6 3.9 %collective-permute-done.2 = bf16[4,1,120,128]{3,2,1,0:T(8,128)(2,1)S(1)} collective-permute-done((bf16[4,1,120,128]{3,2,1,0:T(8,128)(2,1)S(1)}, bf16[4,1,120,128]{3,2,1,0:T(8,128)(2,1)S(1)}, u32[]{:S(2)}, u32[]{:S(2)}) %collective-permute-start.2) | collective-permute-done | bytes 122912 | tf_op jit(solution)/shard_map/ppermute | solution.py:21
  27.8 0.6 fusion.51
  33.1 4.4 %collective-permute-start.3 = (bf16[2,4,120,128]{3,2,1,0:T(8,128)(2,1)S(1)}, bf16[2,4,120,128]{3,2,1,0:T(8,128)(2,1)S(1)}, u32[]{:S(2)}, u32[]{:S(2)}) collective-permute-start(bf16[2,4,120,128]{3,2,1,0:T(8,128)(2,1)S(1)} %multiply_convert_fusion.1), channel_id=1, source_target_pairs={{0,16},{16,32},{32,48},{48,64},{64,80},{80,96},{96,112},{112,128},... | collective-permute-start | bytes 737288 | tf_op jit(solution)/shard_map/ppermute | solution.py:10
  37.5 3.1 %collective-permute-done.3 = bf16[2,4,120,128]{3,2,1,0:T(8,128)(2,1)S(1)} collective-permute-done((bf16[2,4,120,128]{3,2,1,0:T(8,128)(2,1)S(1)}, bf16[2,4,120,128]{3,2,1,0:T(8,128)(2,1)S(1)}, u32[]{:S(2)}, u32[]{:S(2)}) %collective-permute-start.3) | collective-permute-done | bytes 245792 | tf_op jit(solution)/shard_map/ppermute | solution.py:10
  40.6 3.1 %collective-permute-start.4 = (bf16[4,1,120,128]{3,2,1,0:T(8,128)(2,1)S(1)}, bf16[4,1,120,128]{3,2,1,0:T(8,128)(2,1)S(1)}, u32[]{:S(2)}, u32[]{:S(2)}) collective-permute-start(bf16[4,1,120,128]{3,2,1,0:T(8,128)(2,1)S(1)} %get-tuple-element.78), channel_id=1, source_target_pairs={{0,1},{1,2},{2,3},{3,4},{4,5},{5,6},{6,7},{7,8},{8,9},{9,10},{10,1... | collective-permute-start | bytes 368648 | tf_op jit(solution)/shard_map/ppermute | solution.py:20
  43.8 1.3 collective-permute-start.5
  45.6 8.3 %collective-permute-done.5 = bf16[4,1,120,128]{3,2,1,0:T(8,128)(2,1)S(1)} collective-permute-done((bf16[4,1,120,128]{3,2,1,0:T(8,128)(2,1)S(1)}, bf16[4,1,120,128]{3,2,1,0:T(8,128)(2,1)S(1)}, u32[]{:S(2)}, u32[]{:S(2)}) %collective-permute-start.5) | collective-permute-done | bytes 122912 | tf_op jit(solution)/shard_map/ppermute | solution.py:21
  54.5 0.6 fusion.50
  60.4 0.9 fusion.52
  61.6 0.5 all-gather.3.cloned.1.call-update
  62.2 96.7 %all-gather.5.cloned.1.call-done = bf16[64,480,128]{2,1,0:T(8,128)(2,1)} async-done(((bf16[2,480,128]{2,1,0:T(8,128)(2,1)}), bf16[64,480,128]{2,1,0:T(8,128)(2,1)}) %all-gather.5.cloned.1.call-update) | async-done | bytes 7864336 | tf_op jit(solution)/shard_map/all_gather | solution.py:112
  158.9 7.5 %select_reduce_fusion = (f32[2,480]{0,1:T(8,128)S(1)}, f32[2,64,480]{1,0,2:T(2,128)S(1)}) fusion(pred[2,64]{1,0:T(4,128)(4,1)S(1)} %iota_compare_fusion.2, bf16[2,480,128]{2,1,0:T(8,128)(2,1)S(1)} %bitcast.133, bf16[64,480,128]{2,1,0:T(8,128)(2,1)} %all-gather.5.cloned.1.call-done), kind=kOutput, calls=%fused_computation.81 | convolution fusion | flops 15912000 | bytes 8359808 | tf_op jit(solution)/shard_map/fpc,gpc->fgp/dot_general | solution.py:52
  166.5 1.5 fusion.44
  168.1 65.8 %all-gather.3.cloned.1.call-done = bf16[64,480,128]{2,1,0:T(8,128)(2,1)} async-done(((bf16[2,480,128]{2,1,0:T(8,128)(2,1)}), bf16[64,480,128]{2,1,0:T(8,128)(2,1)}) %all-gather.3.cloned.1.call-update) | async-done | bytes 7864336 | tf_op jit(solution)/shard_map/all_gather | solution.py:113
  233.9 6.1 %fusion = f32[480,128,2]{1,2,0:T(2,128)S(1)} fusion(bf16[64,480,128]{2,1,0:T(8,128)(2,1)} %all-gather.3.cloned.1.call-done, f32[2,64,480]{1,0,2:T(2,128)S(1)} %get-tuple-element.91, pred[2,64]{1,0:T(4,128)(4,1)S(1)} %iota_compare_fusion.2, f32[2,480]{0,1:T(8,128)S(1)} %broadcast_maximum_fusion), kind=kOutput, calls=%fused_computation | convolution fusion | flops 15912960 | bytes 8605568 | tf_op jit(solution)/shard_map/fgp,gpc->fpc/dot_general | solution.py:68
  240.2 0.9 fusion.5
  (73 shorter events, 11.7 us)
Async XLA Ops:
  6.5 233.6 %copy-start = (bf16[128,128]{1,0:T(8,128)(2,1)S(1)}, bf16[128,128]{1,0:T(8,128)(2,1)}, u32[]{:S(2)}) copy-start(bf16[128,128]{1,0:T(8,128)(2,1)} %param.17) | copy-start | bytes 98308
  6.5 15.3 %copy-start.2 = (bf16[3,3,3,128,128]{4,3,2,1,0:T(8,128)(2,1)S(1)}, bf16[3,3,3,128,128]{4,3,2,1,0:T(8,128)(2,1)}, u32[]{:S(2)}) copy-start(bf16[3,3,3,128,128]{4,3,2,1,0:T(8,128)(2,1)} %param.11) | copy-start | bytes 2654212
  6.5 152.4 %all-gather.5.cloned.1.call-start = ((), (), s32[]{:S(2)}) async-start(), calls=%async_computation.1 | async-start | bytes 8110080 | tf_op jit(solution)/shard_map/all_gather | solution.py:112
  9.6 9.2 %collective-permute-start = (bf16[2,4,120,128]{3,2,1,0:T(8,128)(2,1)S(1)}, bf16[2,4,120,128]{3,2,1,0:T(8,128)(2,1)S(1)}, u32[]{:S(2)}, u32[]{:S(2)}) collective-permute-start(bf16[2,4,120,128]{3,2,1,0:T(8,128)(2,1)S(1)} %fusion.33), channel_id=1, source_target_pairs={{0,16},{16,32},{32,48},{48,64},{64,80},{80,96},{96,112},{112,128},... | collective-permute-start | bytes 737288 | tf_op jit(solution)/shard_map/ppermute | solution.py:10
  18.8 4.8 %collective-permute-start.1 = (bf16[4,1,120,128]{3,2,1,0:T(8,128)(2,1)S(1)}, bf16[4,1,120,128]{3,2,1,0:T(8,128)(2,1)S(1)}, u32[]{:S(2)}, u32[]{:S(2)}) collective-permute-start(bf16[4,1,120,128]{3,2,1,0:T(8,128)(2,1)S(1)} %get-tuple-element.82), channel_id=1, source_target_pairs={{0,1},{1,2},{2,3},{3,4},{4,5},{5,6},{6,7},{7,8},{8,9},{9,10},{10,1... | collective-permute-start | bytes 368648 | tf_op jit(solution)/shard_map/ppermute | solution.py:20
  20.5 7.0 %collective-permute-start.2 = (bf16[4,1,120,128]{3,2,1,0:T(8,128)(2,1)S(1)}, bf16[4,1,120,128]{3,2,1,0:T(8,128)(2,1)S(1)}, u32[]{:S(2)}, u32[]{:S(2)}) collective-permute-start(bf16[4,1,120,128]{3,2,1,0:T(8,128)(2,1)S(1)} %get-tuple-element.83), channel_id=1, source_target_pairs={{1,0},{2,1},{3,2},{4,3},{5,4},{6,5},{7,6},{8,7},{9,8},{10,9},{11,1... | collective-permute-start | bytes 368648 | tf_op jit(solution)/shard_map/ppermute | solution.py:21
  32.5 12.5 %copy-start.3 = (bf16[3,3,3,128,128]{4,3,2,1,0:T(8,128)(2,1)S(1)}, bf16[3,3,3,128,128]{4,3,2,1,0:T(8,128)(2,1)}, u32[]{:S(2)}) copy-start(bf16[3,3,3,128,128]{4,3,2,1,0:T(8,128)(2,1)} %param.12) | copy-start | bytes 2654212
  32.9 12.3 %copy-start.7 = (bf16[128]{0:T(256)(128)(2,1)S(1)}, bf16[128]{0:T(256)(128)(2,1)}, u32[]{:S(2)}) copy-start(bf16[128]{0:T(256)(128)(2,1)} %param.13) | copy-start | bytes 772
  33.1 7.5 %collective-permute-start.3 = (bf16[2,4,120,128]{3,2,1,0:T(8,128)(2,1)S(1)}, bf16[2,4,120,128]{3,2,1,0:T(8,128)(2,1)S(1)}, u32[]{:S(2)}, u32[]{:S(2)}) collective-permute-start(bf16[2,4,120,128]{3,2,1,0:T(8,128)(2,1)S(1)} %multiply_convert_fusion.1), channel_id=1, source_target_pairs={{0,16},{16,32},{32,48},{48,64},{64,80},{80,96},{96,112},{112,128},... | collective-permute-start | bytes 737288 | tf_op jit(solution)/shard_map/ppermute | solution.py:10
  40.6 5.0 %collective-permute-start.4 = (bf16[4,1,120,128]{3,2,1,0:T(8,128)(2,1)S(1)}, bf16[4,1,120,128]{3,2,1,0:T(8,128)(2,1)S(1)}, u32[]{:S(2)}, u32[]{:S(2)}) collective-permute-start(bf16[4,1,120,128]{3,2,1,0:T(8,128)(2,1)S(1)} %get-tuple-element.78), channel_id=1, source_target_pairs={{0,1},{1,2},{2,3},{3,4},{4,5},{5,6},{6,7},{7,8},{8,9},{9,10},{10,1... | collective-permute-start | bytes 368648 | tf_op jit(solution)/shard_map/ppermute | solution.py:20
  43.8 10.2 %collective-permute-start.5 = (bf16[4,1,120,128]{3,2,1,0:T(8,128)(2,1)S(1)}, bf16[4,1,120,128]{3,2,1,0:T(8,128)(2,1)S(1)}, u32[]{:S(2)}, u32[]{:S(2)}) collective-permute-start(bf16[4,1,120,128]{3,2,1,0:T(8,128)(2,1)S(1)} %get-tuple-element.79), channel_id=1, source_target_pairs={{1,0},{2,1},{3,2},{4,3},{5,4},{6,5},{7,6},{8,7},{9,8},{10,9},{11,1... | collective-permute-start | bytes 368648 | tf_op jit(solution)/shard_map/ppermute | solution.py:21
  58.6 0.9 copy-start.1
  59.0 1.0 copy-start.4
  59.0 1.0 copy-start.5
  59.0 1.0 copy-start.6
  61.3 172.5 %all-gather.3.cloned.1.call-start = ((), (), s32[]{:S(2)}) async-start(), calls=%async_computation | async-start | bytes 8110080 | tf_op jit(solution)/shard_map/all_gather | solution.py:113
Sparse Core Ops, SparseCore 0:
  61.4 97.4 all-gather.4
  161.1 72.7 all-gather.2
where the time goes:
time: 248 us
  waiting for transfers between devices  185 us (75%)
  matrix products  21.2 us (9%)
  starting transfers between devices  16.6 us (7%)
  between operations  14 us (6%)
  other arithmetic  8.13 us (3%)
  local copies, waits for them, and re-layouts  2.88 us (1%)
    all_gather x1, waiting for transfers between devices, local(): lax.all_gather(keys, 'tm', axis=0, tiled=True)  96.7 us
    all_gather x1, waiting for transfers between devices, local(): lax.all_gather(values, 'tm', axis=0, tiled=True)  65.8 us
    ppermute x2, waiting for transfers between devices, with_halo(): after = lax.ppermute(leading, axis, down)  12.2 us
    ppermute x2, starting transfers between devices, shifted(): lax.ppermute(value, axis, [(source, source + steps) for source in range(l...  9.02 us
    ppermute x2, waiting for transfers between devices, shifted(): lax.ppermute(value, axis, [(source, source + steps) for source in range(l...  7.68 us
    dot_general x1, matrix products, block_scores(): jnp.einsum('fpc,gpc->fgp', query, keys, preferred_element_type=jnp.float32)  7.5 us
    dot_general x18, matrix products, convolve(): jnp.dot(joined.reshape(-1, 3 * chans), taps, preferred_element_type=jnp.f...  6.36 us
    dot_general x1, matrix products, absorb_block(): jnp.einsum('fgp,gpc->fpc', weights.astype(jnp.bfloat16), values, preferre...  6.08 us
  transfers between devices with their start and end apart: 8, of which 8 were waited for; matrix products, arithmetic and copies ran while one was open for 4% of the time, Pallas kernels for 0%

commit v1 on v0

--- a/solution.py
+++ b/solution.py
@@ -110,7 +110,9 @@
         start_carry(frames, cells, chans),
         query,
         lax.all_gather(keys, "tm", axis=0, tiled=True),
-        lax.all_gather(values, "tm", axis=0, tiled=True),
+        jnp.concatenate(
+            lax.all_to_all(jnp.stack([values] * lax.axis_size("tm")), "tm", 0, 0), axis=0
+        ),
         query_first,
     )
     mixed = (acc / total[:, :, None]).astype(jnp.bfloat16)

time: 248 us -> 334 us (1.35)
  the two profiles are of different devices: /device:TPU:1 before, /device:TPU:6 now
where the time goes in v1:
time: 334 us
  waiting for transfers between devices  225 us (67%)
  starting transfers between devices  49 us (15%)
  local copies, waits for them, and re-layouts  20.7 us (6%)
  matrix products  17.3 us (5%)
  between operations  14 us (4%)
  other arithmetic  8.13 us (2%)
    all_gather x1, waiting for transfers between devices, local(): lax.all_gather(keys, 'tm', axis=0, tiled=True)  176 us
    all_to_all x1, starting transfers between devices, local(): lax.all_to_all(jnp.stack([values] * lax.axis_size('tm')), 'tm', 0, 0)  26.1 us
    all_to_all x1, waiting for transfers between devices, local(): lax.all_to_all(jnp.stack([values] * lax.axis_size('tm')), 'tm', 0, 0)  25.9 us
    ppermute x2, waiting for transfers between devices, with_halo(): after = lax.ppermute(leading, axis, down)  18.3 us
    ppermute x2, starting transfers between devices, with_halo(): before = lax.ppermute(last, axis, up)  10.9 us
    all_to_all x1, local copies, waits for them, and re-layouts, local(): lax.all_to_all(jnp.stack([values] * lax.axis_size('tm')), 'tm', 0, 0)  9.54 us
    another operation x2, local copies, waits for them, and re-layouts, local(): jnp.stack([values] * lax.axis_size('tm'))  8.38 us
    dot_general x1, matrix products, block_scores(): jnp.einsum('fpc,gpc->fgp', query, keys, preferred_element_type=jnp.float32)  7.5 us
  transfers between devices with their start and end apart: 8, of which 8 were waited for; matrix products, arithmetic and copies ran while one was open for 3% of the time, Pallas kernels for 0%

profile of v1, /device:TPU:6, one launch (start us, length us, event | category | flops | bytes accessed | tf_op | source)
XLA Modules:
  0.0 333.8 jit_solution(18140199567241157185)
XLA Ops:
  6.5 0.7 convert_element_type.47
  7.3 1.2 fusion.24
  8.5 1.2 fusion.31
  9.6 1.8 collective-permute-start
  11.4 1.1 collective-permute-done
  12.5 9.0 %collective-permute-start.1 = (bf16[4,1,120,128]{3,2,1,0:T(8,128)(2,1)S(1)}, bf16[4,1,120,128]{3,2,1,0:T(8,128)(2,1)S(1)}, u32[]{:S(2)}, u32[]{:S(2)}) collective-permute-start(bf16[4,1,120,128]{3,2,1,0:T(8,128)(2,1)S(1)} %get-tuple-element.82), channel_id=1, source_target_pairs={{0,1},{1,2},{2,3},{3,4},{4,5},{5,6},{6,7},{7,8},{8,9},{9,10},{10,1... | collective-permute-start | bytes 368648 | tf_op jit(solution)/shard_map/ppermute | solution.py:20
  21.5 1.9 collective-permute-start.2
  24.0 10.4 %collective-permute-done.2 = bf16[4,1,120,128]{3,2,1,0:T(8,128)(2,1)S(1)} collective-permute-done((bf16[4,1,120,128]{3,2,1,0:T(8,128)(2,1)S(1)}, bf16[4,1,120,128]{3,2,1,0:T(8,128)(2,1)S(1)}, u32[]{:S(2)}, u32[]{:S(2)}) %collective-permute-start.2) | collective-permute-done | bytes 122912 | tf_op jit(solution)/shard_map/ppermute | solution.py:21
  39.9 4.3 %collective-permute-start.3 = (bf16[2,4,120,128]{3,2,1,0:T(8,128)(2,1)S(1)}, bf16[2,4,120,128]{3,2,1,0:T(8,128)(2,1)S(1)}, u32[]{:S(2)}, u32[]{:S(2)}) collective-permute-start(bf16[2,4,120,128]{3,2,1,0:T(8,128)(2,1)S(1)} %multiply_convert_fusion.1), channel_id=1, source_target_pairs={{0,16},{16,32},{32,48},{48,64},{64,80},{80,96},{96,112},{112,128},... | collective-permute-start | bytes 737288 | tf_op jit(solution)/shard_map/ppermute | solution.py:10
  44.2 1.1 collective-permute-done.3
  45.4 1.9 collective-permute-start.4
  47.3 3.9 %collective-permute-start.5 = (bf16[4,1,120,128]{3,2,1,0:T(8,128)(2,1)S(1)}, bf16[4,1,120,128]{3,2,1,0:T(8,128)(2,1)S(1)}, u32[]{:S(2)}, u32[]{:S(2)}) collective-permute-start(bf16[4,1,120,128]{3,2,1,0:T(8,128)(2,1)S(1)} %get-tuple-element.79), channel_id=1, source_target_pairs={{1,0},{2,1},{3,2},{4,3},{5,4},{6,5},{7,6},{8,7},{9,8},{10,9},{11,1... | collective-permute-start | bytes 368648 | tf_op jit(solution)/shard_map/ppermute | solution.py:21
  51.3 0.8 collective-permute-done.4
  52.1 7.9 %collective-permute-done.5 = bf16[4,1,120,128]{3,2,1,0:T(8,128)(2,1)S(1)} collective-permute-done((bf16[4,1,120,128]{3,2,1,0:T(8,128)(2,1)S(1)}, bf16[4,1,120,128]{3,2,1,0:T(8,128)(2,1)S(1)}, u32[]{:S(2)}, u32[]{:S(2)}) %collective-permute-start.5) | collective-permute-done | bytes 122912 | tf_op jit(solution)/shard_map/ppermute | solution.py:21
  66.5 0.8 fusion.51
  67.5 8.2 %stack.3 = bf16[32,2,480,128]{3,1,2,0:T(2,128)(2,1)} broadcast(bf16[2,480,128]{2,0,1:T(2,128)(2,1)S(1)} %copy.27), dimensions={1,2,3} | broadcast | bytes 8110080 | tf_op jit(solution)/shard_map/stack | solution.py:114
  75.7 26.1 %all-to-all-start = ((bf16[32,2,480,128]{3,1,2,0:T(2,128)(2,1)}), bf16[32,2,480,128]{3,1,2,0:T(2,128)(2,1)}, u32[]{:S(2)}, u32[]{:S(2)}) async-start(bf16[32,2,480,128]{3,1,2,0:T(2,128)(2,1)} %stack.3), calls=%async_computation | async-start | bytes 15728640 | tf_op jit(solution)/shard_map/all_to_all | solution.py:114
  102.7 176.3 %all-gather.2.cloned.1.call-done = bf16[64,480,128]{2,1,0:T(8,128)(2,1)} async-done(((bf16[2,480,128]{2,1,0:T(8,128)(2,1)}), bf16[64,480,128]{2,1,0:T(8,128)(2,1)}) %all-gather.2.cloned.1.call-update) | async-done | bytes 7864336 | tf_op jit(solution)/shard_map/all_gather | solution.py:112
  279.0 7.5 %select_reduce_fusion = (f32[2,480]{0,1:T(8,128)S(1)}, f32[2,64,480]{1,0,2:T(2,128)S(1)}) fusion(pred[2,64]{1,0:T(4,128)(4,1)S(1)} %iota_compare_fusion.2, bf16[2,480,128]{2,1,0:T(8,128)(2,1)S(1)} %bitcast.136, bf16[64,480,128]{2,1,0:T(8,128)(2,1)} %all-gather.2.cloned.1.call-done), kind=kOutput, calls=%fused_computation.79 | convolution fusion | flops 15912000 | bytes 8359808 | tf_op jit(solution)/shard_map/fpc,gpc->fgp/dot_general | solution.py:52
  286.5 1.5 fusion.43
  288.2 25.9 %all-to-all-done = bf16[32,2,480,128]{3,1,2,0:T(2,128)(2,1)} async-done(((bf16[32,2,480,128]{3,1,2,0:T(2,128)(2,1)}), bf16[32,2,480,128]{3,1,2,0:T(2,128)(2,1)}, u32[]{:S(2)}, u32[]{:S(2)}) %all-to-all-start) | async-done | bytes 7864352 | tf_op jit(solution)/shard_map/all_to_all | solution.py:114
  314.1 9.5 %copy.28 = bf16[32,2,480,128]{3,1,0,2:T(2,128)(2,1)S(1)} copy(bf16[32,2,480,128]{3,1,2,0:T(2,128)(2,1)} %all-to-all-done) | data formatting | bytes 15728640 | tf_op jit(solution)/shard_map/all_to_all | solution.py:114
  323.6 2.2 fusion.36
  326.1 0.9 fusion.3
  (75 shorter events, 13.5 us)
Async XLA Ops:
  6.5 319.5 %copy-start = (bf16[128,128]{1,0:T(8,128)(2,1)S(1)}, bf16[128,128]{1,0:T(8,128)(2,1)}, u32[]{:S(2)}) copy-start(bf16[128,128]{1,0:T(8,128)(2,1)} %param.17) | copy-start | bytes 98308
  6.5 16.9 %copy-start.2 = (bf16[3,3,3,128,128]{4,3,2,1,0:T(8,128)(2,1)S(1)}, bf16[3,3,3,128,128]{4,3,2,1,0:T(8,128)(2,1)}, u32[]{:S(2)}) copy-start(bf16[3,3,3,128,128]{4,3,2,1,0:T(8,128)(2,1)} %param.11) | copy-start | bytes 2654212
  9.6 2.9 collective-permute-start
  12.5 11.4 %collective-permute-start.1 = (bf16[4,1,120,128]{3,2,1,0:T(8,128)(2,1)S(1)}, bf16[4,1,120,128]{3,2,1,0:T(8,128)(2,1)S(1)}, u32[]{:S(2)}, u32[]{:S(2)}) collective-permute-start(bf16[4,1,120,128]{3,2,1,0:T(8,128)(2,1)S(1)} %get-tuple-element.82), channel_id=1, source_target_pairs={{0,1},{1,2},{2,3},{3,4},{4,5},{5,6},{6,7},{7,8},{8,9},{9,10},{10,1... | collective-permute-start | bytes 368648 | tf_op jit(solution)/shard_map/ppermute | solution.py:20
  21.5 12.8 %collective-permute-start.2 = (bf16[4,1,120,128]{3,2,1,0:T(8,128)(2,1)S(1)}, bf16[4,1,120,128]{3,2,1,0:T(8,128)(2,1)S(1)}, u32[]{:S(2)}, u32[]{:S(2)}) collective-permute-start(bf16[4,1,120,128]{3,2,1,0:T(8,128)(2,1)S(1)} %get-tuple-element.83), channel_id=1, source_target_pairs={{1,0},{2,1},{3,2},{4,3},{5,4},{6,5},{7,6},{8,7},{9,8},{10,9},{11,1... | collective-permute-start | bytes 368648 | tf_op jit(solution)/shard_map/ppermute | solution.py:21
  39.3 11.9 %copy-start.3 = (bf16[3,3,3,128,128]{4,3,2,1,0:T(8,128)(2,1)S(1)}, bf16[3,3,3,128,128]{4,3,2,1,0:T(8,128)(2,1)}, u32[]{:S(2)}) copy-start(bf16[3,3,3,128,128]{4,3,2,1,0:T(8,128)(2,1)} %param.12) | copy-start | bytes 2654212
  39.7 11.6 %copy-start.7 = (bf16[128]{0:T(256)(128)(2,1)S(1)}, bf16[128]{0:T(256)(128)(2,1)}, u32[]{:S(2)}) copy-start(bf16[128]{0:T(256)(128)(2,1)} %param.13) | copy-start | bytes 772
  39.9 5.5 %collective-permute-start.3 = (bf16[2,4,120,128]{3,2,1,0:T(8,128)(2,1)S(1)}, bf16[2,4,120,128]{3,2,1,0:T(8,128)(2,1)S(1)}, u32[]{:S(2)}, u32[]{:S(2)}) collective-permute-start(bf16[2,4,120,128]{3,2,1,0:T(8,128)(2,1)S(1)} %multiply_convert_fusion.1), channel_id=1, source_target_pairs={{0,16},{16,32},{32,48},{48,64},{64,80},{80,96},{96,112},{112,128},... | collective-permute-start | bytes 737288 | tf_op jit(solution)/shard_map/ppermute | solution.py:10
  45.4 6.8 %collective-permute-start.4 = (bf16[4,1,120,128]{3,2,1,0:T(8,128)(2,1)S(1)}, bf16[4,1,120,128]{3,2,1,0:T(8,128)(2,1)S(1)}, u32[]{:S(2)}, u32[]{:S(2)}) collective-permute-start(bf16[4,1,120,128]{3,2,1,0:T(8,128)(2,1)S(1)} %get-tuple-element.78), channel_id=1, source_target_pairs={{0,1},{1,2},{2,3},{3,4},{4,5},{5,6},{6,7},{7,8},{8,9},{9,10},{10,1... | collective-permute-start | bytes 368648 | tf_op jit(solution)/shard_map/ppermute | solution.py:20
  47.3 12.8 %collective-permute-start.5 = (bf16[4,1,120,128]{3,2,1,0:T(8,128)(2,1)S(1)}, bf16[4,1,120,128]{3,2,1,0:T(8,128)(2,1)S(1)}, u32[]{:S(2)}, u32[]{:S(2)}) collective-permute-start(bf16[4,1,120,128]{3,2,1,0:T(8,128)(2,1)S(1)} %get-tuple-element.79), channel_id=1, source_target_pairs={{1,0},{2,1},{3,2},{4,3},{5,4},{6,5},{7,6},{8,7},{9,8},{10,9},{11,1... | collective-permute-start | bytes 368648 | tf_op jit(solution)/shard_map/ppermute | solution.py:21
  64.7 0.9 copy-start.1
  65.1 1.0 copy-start.4
  65.1 1.0 copy-start.5
  65.1 1.0 copy-start.6
  75.7 238.4 %all-to-all-start = ((bf16[32,2,480,128]{3,1,2,0:T(2,128)(2,1)}), bf16[32,2,480,128]{3,1,2,0:T(2,128)(2,1)}, u32[]{:S(2)}, u32[]{:S(2)}) async-start(bf16[32,2,480,128]{3,1,2,0:T(2,128)(2,1)} %stack.3), calls=%async_computation | async-start | bytes 15728640 | tf_op jit(solution)/shard_map/all_to_all | solution.py:114
  101.8 177.2 %all-gather.2.cloned.1.call-start = ((), (), s32[]{:S(2)}) async-start(), calls=%async_computation.1 | async-start | bytes 8110080 | tf_op jit(solution)/shard_map/all_gather | solution.py:112
Sparse Core Ops, SparseCore 0:
  104.8 174.1 all-gather.1
